TPU v7x, 32 devices: a whole 2x2x4 slice. The times are simulated.
32 devices in a mesh: groups: 2 (over x), shard: 16 (over z, y, core).
Axes of the slice: x: 2, y: 2, z: 4, core: 2. Of those that a mesh axis runs over, the one named last changes fastest.
Arguments:
- residual_in: bfloat16 [128, 5120], P('groups', 'shard'), parts along dimension 0, may hold values from -12 to 12
- queries: bfloat16 [64, 16, 640], P(('groups', 'shard')), parts along dimension 0, may hold values from -8 to 8
- key_cache: bfloat16 [64, 4096, 128], P(('groups', 'shard')), parts along dimension 0, may hold values from -6 to 6
- value_cache: bfloat16 [64, 4096, 128], P(('groups', 'shard')), parts along dimension 0, may hold values from -6 to 6
- new_keys: bfloat16 [64, 16, 128], P(('groups', 'shard')), parts along dimension 0, may hold values from -8 to 8
- new_values: bfloat16 [64, 16, 128], P(('groups', 'shard')), parts along dimension 0, may hold values from -6 to 6
- cache_len: int32 [8], P('groups'), parts along dimension 0, may hold values from 1024 to 4096, as said below
- tree_mask: int32 [8, 16, 16], P('groups'), parts along dimension 0, may hold values from 0 to 1, as said below
- out_proj: bfloat16 [5120, 5120], P(None, 'shard'), may hold values from -0.25 to 0.25
- norm_gain: bfloat16 [5120], P('shard'), may hold values from 0.099609375 to 1.8984375
- gate_w: bfloat16 [5120, 27648], P(None, 'shard'), may hold values from -0.078125 to 0.078125
- up_w: bfloat16 [5120, 27648], P(None, 'shard'), may hold values from -0.078125 to 0.078125
- down_w: bfloat16 [27648, 5120], P('shard'), may hold values from -0.0390625 to 0.0390625
Outputs:
- layer_out: bfloat16 [128, 5120], P(('groups', 'shard')), parts along dimension 0
There are 2 independent parts, one for each index of `groups`. A program takes and returns all parts, laid end to end along the dimension named above; an argument that names none is the same for every part. Nothing has to cross between parts.
Inputs may be any that keep to these rules, and one draw needn't show every extreme that they name: Positions 0 to cache_len[r] - 1 of request r's blocks are valid; some request fills all 4096 positions. tree_mask[r, i, j] is 1 exactly where draft row j is row i itself or an ancestor of row i in request r's draft tree; a row's parent comes before it, and row 0 is the root.
All inputs are finite; a program needn't handle non-finite values.
Results may differ from a plain program's by a relative error of at most 0.0059.
Values may be sent and summed in bfloat16 or wider, within the bound.
A program may use at most 128 MiB of HBM per device.

v0:
```python
import math

import jax
import jax.numpy as jnp
from jax import lax
from jax.sharding import PartitionSpec as P

D = 5120
KV = 8
HD = 128
G = 5


def on_device(
    residual_in,
    queries,
    key_cache,
    value_cache,
    new_keys,
    new_values,
    cache_len,
    tree_mask,
    out_proj,
    norm_gain,
    gate_w,
    up_w,
    down_w,
):
    blocks = queries.shape[0]
    drafts = queries.shape[1]
    requests = cache_len.shape[0]
    row_count = requests * drafts
    first_pair = lax.axis_index("shard") * blocks
    pair_index = first_pair + jnp.arange(blocks, dtype=jnp.int32)
    req_index = pair_index % requests
    req_pick = (req_index[:, None] == jnp.arange(requests, dtype=jnp.int32)[None, :]).astype(
        jnp.int32
    )
    lengths = jnp.sum(req_pick * cache_len[None, :], axis=1)
    tree_rows = jnp.einsum("br,rij->bij", req_pick, tree_mask)
    head_rows = queries.reshape(blocks, drafts, G, HD)
    score_scale = 1.0 / math.sqrt(HD)
    cache_scores = (
        jnp.einsum("bdgk,blk->bdgl", head_rows, key_cache, preferred_element_type=jnp.float32)
        * score_scale
    )
    draft_scores = (
        jnp.einsum("bdgk,bek->bdge", head_rows, new_keys, preferred_element_type=jnp.float32)
        * score_scale
    )
    valid_keys = jnp.arange(key_cache.shape[1], dtype=jnp.int32)[None, :] < lengths[:, None]
    cache_scores = jnp.where(valid_keys[:, None, None, :], cache_scores, -1e30)
    draft_scores = jnp.where(tree_rows[:, :, None, :] > 0, draft_scores, -1e30)
    peak_score = jnp.maximum(jnp.max(cache_scores, axis=-1), jnp.max(draft_scores, axis=-1))
    cache_weights = jnp.where(
        valid_keys[:, None, None, :], jnp.exp(cache_scores - peak_score[..., None]), 0.0
    )
    draft_weights = jnp.where(
        tree_rows[:, :, None, :] > 0, jnp.exp(draft_scores - peak_score[..., None]), 0.0
    )
    denom = jnp.sum(cache_weights, axis=-1) + jnp.sum(draft_weights, axis=-1)
    weighted = jnp.einsum(
        "bdgl,blk->bdgk",
        cache_weights.astype(jnp.bfloat16),
        value_cache,
        preferred_element_type=jnp.float32,
    )
    weighted = weighted + jnp.einsum(
        "bdge,bek->bdgk",
        draft_weights.astype(jnp.bfloat16),
        new_values,
        preferred_element_type=jnp.float32,
    )
    attn = (weighted / denom[..., None]).astype(jnp.bfloat16).reshape(blocks, drafts, G * HD)
    col_width = out_proj.shape[1]
    head_projection = out_proj.reshape(KV, G * HD, col_width)
    share_slice = lax.all_gather(attn, "shard", axis=0, tiled=True)
    taken = share_slice.shape[0]
    pair_ids = jnp.arange(taken, dtype=jnp.int32)
    head_selection = (
        pair_ids[:, None] // requests == jnp.arange(KV, dtype=jnp.int32)[None, :]
    ).astype(jnp.bfloat16)
    row_pick = (
        pair_ids[:, None] % requests == jnp.arange(requests, dtype=jnp.int32)[None, :]
    ).astype(jnp.float32)
    selected_entry = jnp.einsum(
        "ji,itq->jtq", head_selection, head_projection, preferred_element_type=jnp.float32
    ).astype(jnp.bfloat16)
    projected_rows = jnp.einsum(
        "wgr,wrb->wgb", share_slice, selected_entry, preferred_element_type=jnp.float32
    )
    mixed = jnp.einsum("pr,pdc->rdc", row_pick, projected_rows, precision=lax.Precision.HIGHEST)
    stream = (residual_in.astype(jnp.float32) + mixed.reshape(row_count, col_width)).astype(
        jnp.bfloat16
    )
    wide_local = stream.astype(jnp.float32)
    squares = lax.psum(jnp.sum(wide_local * wide_local, axis=1), "shard")
    inverse = lax.rsqrt(squares / D + 1e-06)
    normed = (wide_local * inverse[:, None] * norm_gain.astype(jnp.float32)[None, :]).astype(
        jnp.bfloat16
    )
    share_slice = lax.all_gather(normed, "shard", axis=1, tiled=True)
    gate_acts = jnp.dot(share_slice, gate_w, preferred_element_type=jnp.float32)
    up_acts = jnp.dot(share_slice, up_w, preferred_element_type=jnp.float32)
    hidden = (jax.nn.silu(gate_acts) * up_acts).astype(jnp.bfloat16)
    summed_cols = lax.psum_scatter(
        lax.dot_general(
            down_w, hidden, (((0,), (1,)), ((), ())), preferred_element_type=jnp.float32
        ),
        "shard",
        scatter_dimension=0,
        tiled=True,
    )
    finished = (stream.astype(jnp.float32) + summed_cols.T).astype(jnp.bfloat16)
    return lax.all_to_all(finished, "shard", split_axis=0, concat_axis=1, tiled=True)


def solution(mesh):
    placed = (
        P("groups", "shard"),
        P(("groups", "shard"), None, None),
        P(("groups", "shard"), None, None),
        P(("groups", "shard"), None, None),
        P(("groups", "shard"), None, None),
        P(("groups", "shard"), None, None),
        P("groups"),
        P("groups", None, None),
        P(None, "shard"),
        P("shard"),
        P(None, "shard"),
        P(None, "shard"),
        P("shard", None),
    )
    return jax.shard_map(
        on_device,
        mesh=mesh,
        in_specs=placed,
        out_specs=P(("groups", "shard"), None),
        check_vma=False,
    )
```

profile of v0, /device:TPU:0, one launch (start us, length us, event | category | flops | bytes accessed | tf_op | source)
XLA Modules:
  0.0 218.1 jit_solution(16136266303252166860)
XLA Ops:
  6.5 0.0 copy-start
  6.5 0.0 copy-start.4
  6.5 0.0 copy-start.6
  6.5 0.0 reduce-scatter.4.cloned.1.call-start
  6.6 1.0 select_reduce_fusion
  7.6 0.1 iota_compare_fusion
  7.7 1.0 convolution_compare_fusion
  8.7 0.1 copy.31
  8.8 0.0 copy-done
  8.8 1.7 fusion.57
  10.5 0.0 copy-done.4
  10.5 0.0 copy-done.6
  10.5 0.0 copy-start.3
  10.5 0.2 fusion.58
  10.8 0.6 fusion.4
  11.4 0.7 copy-done.3
  12.1 0.0 copy-start.8
  12.1 0.0 copy-start.2
  12.1 0.7 fusion.6
  12.8 0.0 copy-done.8
  12.8 0.2 fusion.16
  13.0 25.2 %all_gather.6 = bf16[32,16,640]{2,1,0:T(8,128)(2,1)S(1)} all-gather(bf16[2,16,640]{2,1,0:T(8,128)(2,1)S(1)} %bitcast.85), channel_id=1, replica_groups=mesh['groups'=2,'shard'=16] {'shard'}, dimensions={0}, use_global_device_ids=true | all-gather | bytes 696320 | tf_op jit(solution)/shard_map/all_gather | solution.py:77
  38.2 0.0 copy-done.2
  38.2 0.6 copy.49
  38.9 6.6 %convolution_convert_fusion = bf16[32,640,320]{1,0,2:T(8,128)(2,1)} fusion(bf16[8,640,320]{1,0,2:T(8,128)(2,1)S(1)} %bitcast.82, s32[32]{0:T(128)S(1)} %and_select_fusion), kind=kOutput, calls=%fused_computation.2 | convolution fusion | flops 111411456 | bytes 16384128 | tf_op jit(solution)/shard_map/ji,itq->jtq/dot_general | solution.py:86
  45.5 0.0 copy-start.5
  45.5 0.0 copy-start.7
  45.5 10.0 %fusion = f32[32,16,320]{2,1,0:T(8,128)S(1)} fusion(bf16[32,16,640]{2,1,0:T(8,128)(2,1)S(1)} %all_gather.6, bf16[32,640,320]{1,0,2:T(8,128)(2,1)} %convolution_convert_fusion), kind=kOutput, calls=%fused_computation | convolution fusion | flops 209715200 | bytes 14417920 | tf_op jit(solution)/shard_map/wgr,wrb->wgb/dot_general | solution.py:89
  55.4 0.6 fusion.17
  56.1 0.0 copy-done.5
  56.1 0.1 fusion.25
  56.2 29.8 %psum.7 = f32[64]{0:T(128)S(1)} all-reduce(f32[64]{0:T(128)S(1)} %get-tuple-element.5), channel_id=1, replica_groups=mesh['groups'=2,'shard'=16] {'shard'}, use_global_device_ids=true, to_apply=%region_6.7 | all-reduce | flops 64 | bytes 512 | tf_op jit(solution)/shard_map/psum | solution.py:97
  86.0 0.0 copy-done.7
  86.0 0.1 fusion.32
  86.1 19.9 %all-gather = bf16[16,320,64]{1,2,0:T(8,128)(2,1)S(1)} all-gather(bf16[1,320,64]{1,2,0:T(8,128)(2,1)S(1)} %fusion.32), channel_id=1, replica_groups=mesh['groups'=2,'shard'=16] {'shard'}, dimensions={0}, use_global_device_ids=true | all-gather | bytes 696320 | tf_op jit(solution)/shard_map/all_gather | solution.py:102
  106.0 0.5 copy.38
  106.5 0.6 reshape.119
  107.1 11.4 %fusion.59 = f32[64,1728]{1,0:T(8,128)S(1)} fusion(bf16[5120,64]{0,1:T(8,128)(2,1)S(1)} %reshape.119, bf16[5120,1728]{0,1:T(8,128)(2,1)} %param.23), kind=kOutput, calls=%fused_computation.82 | convolution fusion | flops 1132462080 | bytes 18792448 | tf_op jit(solution)/shard_map/dot_general | solution.py:103
  118.5 16.0 %convolution_bitcast_fusion = f32[5120,64]{0,1:T(8,128)S(1)} fusion(bf16[1728,5120]{1,0:T(8,128)(2,1)} %param.25, bf16[5120,64]{0,1:T(8,128)(2,1)S(1)} %reshape.119, bf16[5120,1728]{0,1:T(8,128)(2,1)} %param.24, f32[64,1728]{1,0:T(8,128)S(1)} %fusion.59), kind=kOutput, calls=%fused_computation.3 | convolution fusion | flops 2265587712 | bytes 37797888 | tf_op jit(solution)/shard_map/dot_general | solution.py:107
  134.5 0.0 copy-start.1
  134.5 2.0 copy.45
  136.6 0.0 reduce-scatter.4.cloned.1.call-update
  136.6 62.6 %reduce-scatter.4.cloned.1.call-done = f32[320,64]{1,0:T(8,128)} async-done(((f32[5120,64]{1,0:T(8,128)}), f32[320,64]{1,0:T(8,128)}) %reduce-scatter.4.cloned.1.call-update) | async-done | bytes 81936
  199.2 1.0 copy.46
  200.3 10.2 %all_to_all.19 = bf16[16,4,320]{2,1,0:T(4,128)(2,1)S(1)} all-to-all(bf16[16,4,320]{2,1,0:T(4,128)(2,1)S(1)} %all_to_all.14), channel_id=1, replica_groups=mesh['groups'=2,'shard'=16] {'shard'}, dimensions={0} | all-to-all | bytes 81920 | tf_op jit(solution)/shard_map/all_to_all | solution.py:115
  210.5 0.7 all_to_all.17
  211.2 0.0 copy-done.1
  (13 shorter events, 0.1 us)
Async XLA Ops:
  6.5 2.2 %copy-start = (bf16[2,4096,128]{2,1,0:T(8,128)(2,1)S(1)}, bf16[2,4096,128]{2,1,0:T(8,128)(2,1)}, u32[]{:S(2)}) copy-start(bf16[2,4096,128]{2,1,0:T(8,128)(2,1)} %param.15) | copy-start | bytes 6291460
  6.5 3.9 %copy-start.4 = (bf16[2,16,640]{2,1,0:T(8,128)(2,1)S(1)}, bf16[2,16,640]{2,1,0:T(8,128)(2,1)}, u32[]{:S(2)}) copy-start(bf16[2,16,640]{2,1,0:T(8,128)(2,1)} %param.14) | copy-start | bytes 122884
  6.5 3.9 %copy-start.6 = (bf16[2,16,128]{2,1,0:T(8,128)(2,1)S(1)}, bf16[2,16,128]{2,1,0:T(8,128)(2,1)}, u32[]{:S(2)}) copy-start(bf16[2,16,128]{2,1,0:T(8,128)(2,1)} %param.17) | copy-start | bytes 24580
  6.5 192.6 %reduce-scatter.4.cloned.1.call-start = ((), (), s32[]{:S(2)}) async-start(), calls=%async_computation.2 | async-start | bytes 2785280
  10.5 1.6 copy-start.3
  12.1 0.7 copy-start.8
  12.1 26.2 %copy-start.2 = (bf16[5120,320]{0,1:T(8,128)(2,1)S(1)}, bf16[5120,320]{0,1:T(8,128)(2,1)}, u32[]{:S(2)}) copy-start(bf16[5120,320]{0,1:T(8,128)(2,1)} %param.21) | copy-start | bytes 9830404
  45.5 10.6 %copy-start.5 = (bf16[64,320]{1,0:T(8,128)(2,1)S(1)}, bf16[64,320]{1,0:T(8,128)(2,1)}, u32[]{:S(2)}) copy-start(bf16[64,320]{1,0:T(8,128)(2,1)} %param.13) | copy-start | bytes 122884
  45.5 40.6 %copy-start.7 = (bf16[320]{0:T(512)(128)(2,1)S(1)}, bf16[320]{0:T(512)(128)(2,1)}, u32[]{:S(2)}) copy-start(bf16[320]{0:T(512)(128)(2,1)} %param.22) | copy-start | bytes 1924
  134.5 76.7 %copy-start.1 = (bf16[2,4096,128]{2,1,0:T(8,128)(2,1)S(1)}, bf16[2,4096,128]{2,1,0:T(8,128)(2,1)}, u32[]{:S(2)}) copy-start(bf16[2,4096,128]{2,1,0:T(8,128)(2,1)} %param.15) | copy-start | bytes 6291460
Sparse Core Ops, SparseCore 0:
  136.7 62.4 reduce-scatter.3
where the time goes:
time: 218 us
  blocking collectives  85.2 us (39%)
  waiting for transfers between devices  62.6 us (29%)
  matrix products  48.3 us (22%)
  between operations  13.6 us (6%)
  local copies, waits for them, and re-layouts  6.35 us (3%)
    unnamed x2, waiting for transfers between devices  62.6 us
    psum x1, blocking collectives, on_device(): squares = lax.psum(jnp.sum(wide_local * wide_local, axis=1), 'shard')  29.8 us
    all_gather x1, blocking collectives, on_device(): share_slice = lax.all_gather(attn, 'shard', axis=0, tiled=True)  25.2 us
    all_gather x1, blocking collectives, on_device(): share_slice = lax.all_gather(normed, 'shard', axis=1, tiled=True)  19.9 us
    dot_general x1, matrix products, on_device(): lax.dot_general(down_w, hidden, (((0,), (1,)), ((), ())), preferred_eleme...  16 us
    dot_general x1, matrix products, on_device(): gate_acts = jnp.dot(share_slice, gate_w, preferred_element_type=jnp.float32)  11.4 us
    all_to_all x1, blocking collectives, on_device(): lax.all_to_all(finished, 'shard', split_axis=0, concat_axis=1, tiled=True)  10.2 us
    dot_general x1, matrix products, on_device(): jnp.einsum('wgr,wrb->wgb', share_slice, selected_entry, preferred_element...  9.98 us
  transfers between devices with their start and end apart: 1, of which 1 were waited for; matrix products, arithmetic and copies ran while one was open for 0% of the time, Pallas kernels for 0%

commit v1 on v0

v1 whole, which is shorter than its diff:
```python
import functools
import math

import jax
import jax.numpy as jnp
from jax import lax
from jax.experimental import pallas as pl
from jax.experimental.pallas import tpu as pltpu
from jax.sharding import PartitionSpec as P

HD = 128
G = 5


CORES = 2
EPS = 1e-06


def remote(src, dst, send_sem, recv_sem, target):
    return pltpu.make_async_remote_copy(
        src_ref=src,
        dst_ref=dst,
        send_sem=send_sem,
        recv_sem=recv_sem,
        device_id={"shard": target},
        device_id_type=pl.DeviceIdType.MESH,
    )


def layer_kernel(
    shards,
    requests,
    drafts,
    attn_ref,
    resid_ref,
    gain_ref,
    wo_hbm,
    gate_hbm,
    up_hbm,
    down_hbm,
    out_ref,
    wo,
    gate,
    up,
    down,
    attn_slots,
    gain_slots,
    stream_slots,
    low_rows,
    wide_rows,
    own_rows,
    gains,
    hidden,
    mine_block,
    other_block,
    pair_out,
    pair_in,
    send_blocks,
    recv_blocks,
    weight_sems,
    attn_sems,
    gain_sems,
    stream_sems,
    pair_sems,
    final_sems,
):
    chips = shards // CORES
    me = lax.axis_index("shard")
    chip = me // CORES
    core = me % CORES
    pair = chip * CORES + 1 - core
    rows, depth = low_rows.shape
    width = resid_ref.shape[1]
    out_rows = out_ref.shape[0]
    pieces = down.shape[0]
    total_pieces = depth // down.shape[2]
    piece = down.shape[2]
    chip_rows = out_rows * CORES

    def down_copy(q):
        return pltpu.make_async_copy(
            down_hbm.at[:, pl.ds(q * piece, piece)], down.at[q % pieces], weight_sems.at[3 + q]
        )

    wo_copy = pltpu.make_async_copy(wo_hbm, wo, weight_sems.at[0])
    gate_copy = pltpu.make_async_copy(gate_hbm, gate, weight_sems.at[1])
    up_copy = pltpu.make_async_copy(up_hbm, up, weight_sems.at[2])
    wo_copy.start()
    gate_copy.start()
    up_copy.start()
    for q in range(pieces):
        down_copy(q).start()

    barrier = pltpu.get_barrier_semaphore()

    def greet(j, carry):
        target = ((chip + j) % chips) * CORES + core
        pl.semaphore_signal(
            barrier, inc=1, device_id={"shard": target}, device_id_type=pl.DeviceIdType.MESH
        )
        return carry

    lax.fori_loop(1, chips, greet, 0)
    pl.semaphore_signal(
        barrier, inc=1, device_id={"shard": pair}, device_id_type=pl.DeviceIdType.MESH
    )
    pl.semaphore_wait(barrier, chips)

    def direct(slots, sems, j):
        target = ((chip + j) % chips) * CORES + core
        return remote(slots.at[me], slots.at[me], sems.at[0, j], sems.at[1, chip], target)

    def relay(slots, sems, j):
        origin = (chip + chips - j) % chips
        block = origin * CORES + core
        return remote(slots.at[block], slots.at[block], sems.at[2, j], sems.at[3, origin], pair)

    def gather_start(slots, sems):
        def send(j, carry):
            direct(slots, sems, j).start()
            return carry

        relay(slots, sems, 0).start()
        lax.fori_loop(1, chips, send, 0)

    def gather_finish(slots, sems):
        def forward(j, carry):
            origin = (chip + chips - j) % chips
            block = origin * CORES + core
            remote(
                slots.at[block], slots.at[block], sems.at[0, j], sems.at[1, origin], pair
            ).wait_recv()
            relay(slots, sems, j).start()
            return carry

        def arrive(j, carry):
            origin = (chip + chips - j) % chips
            block = origin * CORES + 1 - core
            remote(
                slots.at[block], slots.at[block], sems.at[2, j], sems.at[3, origin], pair
            ).wait_recv()
            return carry

        lax.fori_loop(1, chips, forward, 0)
        lax.fori_loop(0, chips, arrive, 0)

    def gather_drain(slots, sems):
        def drain(j, carry):
            direct(slots, sems, j).wait_send()
            relay(slots, sems, j).wait_send()
            return carry

        relay(slots, sems, 0).wait_send()
        lax.fori_loop(1, chips, drain, 0)

    attn_slots[me] = attn_ref[...]
    gain_slots[me] = gain_ref[...]
    gather_start(attn_slots, attn_sems)
    gather_start(gain_slots, gain_sems)
    gather_finish(attn_slots, attn_sems)

    blocks = attn_ref.shape[0] // drafts
    head_width = attn_ref.shape[1]
    for p in range(shards * blocks):
        head, request = p // requests, p % requests
        low_rows[
            request * drafts : (request + 1) * drafts, head * head_width : (head + 1) * head_width
        ] = attn_slots[p // blocks, (p % blocks) * drafts : (p % blocks + 1) * drafts, :]
    wo_copy.wait()
    mixed = jnp.dot(low_rows[...], wo[...], preferred_element_type=jnp.float32)
    stream_slots[me] = (resid_ref[...].astype(jnp.float32) + mixed).astype(jnp.bfloat16)
    gather_start(stream_slots, stream_sems)
    gather_finish(gain_slots, gain_sems)
    for s in range(shards):
        gains[:, s * width : (s + 1) * width] = gain_slots[s]
    gather_finish(stream_slots, stream_sems)
    for s in range(shards):
        wide_rows[:, s * width : (s + 1) * width] = stream_slots[s].astype(jnp.float32)
    own_rows[...] = wide_rows[pl.ds(pl.multiple_of(chip * chip_rows, chip_rows), chip_rows), :]

    def norm(i, carry):
        band = pl.ds(pl.multiple_of(i * 16, 16), 16)
        wide = wide_rows[band, :]
        inverse = lax.rsqrt(jnp.sum(wide * wide, axis=1, keepdims=True) / depth + EPS)
        low_rows[band, :] = (wide * inverse * gains[...]).astype(jnp.bfloat16)
        return carry

    lax.fori_loop(0, rows // 16, norm, 0)

    gate_copy.wait()
    up_copy.wait()
    units = gate.shape[1]
    for first in range(0, units, 512):
        last = min(first + 512, units)
        gate_acts = jnp.dot(
            low_rows[...], gate[:, first:last], preferred_element_type=jnp.float32
        )
        up_acts = jnp.dot(low_rows[...], up[:, first:last], preferred_element_type=jnp.float32)
        hidden[:, first:last] = (jax.nn.silu(gate_acts) * up_acts).astype(jnp.bfloat16)

    for q in range(total_pieces):
        down_copy(q).wait()
        wide_rows[:, q * piece : (q + 1) * piece] = jnp.dot(
            hidden[...], down[q % pieces], preferred_element_type=jnp.float32
        )
        if q + pieces < total_pieces:
            down_copy(q + pieces).start()

    def take(c, block, which):
        for q in range(total_pieces):
            both = wide_rows[
                pl.ds(pl.multiple_of(c * chip_rows, chip_rows), chip_rows),
                q * piece : (q + 1) * piece,
            ]
            block[q * out_rows : (q + 1) * out_rows, :] = jnp.where(
                which == 0, both[:out_rows], both[out_rows:]
            )
        return block[...]

    def give(c, carry):
        pair_out[c] = take(c, other_block, 1 - core).astype(jnp.bfloat16)
        return carry

    lax.fori_loop(0, chips, give, 0)
    pair_copy = remote(pair_out, pair_in, pair_sems.at[0], pair_sems.at[1], pair)
    pair_copy.start()
    pair_copy.wait()

    def scatter(j):
        target = (chip + j) % chips
        return remote(
            send_blocks.at[target],
            recv_blocks.at[chip],
            final_sems.at[0, j],
            final_sems.at[1, chip],
            target * CORES + core,
        )

    def combine(j, carry):
        target = (chip + j) % chips
        summed = take(target, mine_block, core) + pair_in[target].astype(jnp.float32)
        send_blocks[target] = summed.astype(jnp.bfloat16)
        scatter(j).start()
        return carry

    lax.fori_loop(1, chips, combine, 0)
    total = take(chip, mine_block, core) + pair_in[chip].astype(jnp.float32)

    def add(j, total):
        origin = (chip + chips - j) % chips
        remote(
            send_blocks.at[origin],
            recv_blocks.at[origin],
            final_sems.at[0, j],
            final_sems.at[1, origin],
            pair,
        ).wait_recv()
        return total + recv_blocks[origin].astype(jnp.float32)

    mine_block[...] = lax.fori_loop(1, chips, add, total)
    for q in range(total_pieces):
        both = own_rows[:, q * piece : (q + 1) * piece]
        stream = jnp.where(core == 0, both[:out_rows], both[out_rows:])
        out_ref[:, q * piece : (q + 1) * piece] = (
            stream + mine_block[q * out_rows : (q + 1) * out_rows, :]
        ).astype(jnp.bfloat16)

    def drain(j, carry):
        scatter(j).wait_send()
        return carry

    lax.fori_loop(1, chips, drain, 0)
    gather_drain(attn_slots, attn_sems)
    gather_drain(gain_slots, gain_sems)
    gather_drain(stream_slots, stream_sems)


def rest_of_layer(shards, requests, drafts, attn, residual_in, norm_gain, *weights):
    rows, width = residual_in.shape
    out_proj, gate_w, up_w, down_w = weights
    depth = out_proj.shape[0]
    units = gate_w.shape[1]
    chips = shards // CORES
    out_rows = rows // shards
    piece = depth * out_rows // 16
    slots = (chips, 16, piece)
    bf16, f32 = jnp.bfloat16, jnp.float32
    vmem, hbm = pl.BlockSpec(memory_space=pltpu.VMEM), pl.BlockSpec(memory_space=pl.ANY)
    dma = pltpu.SemaphoreType.DMA
    return pl.pallas_call(
        functools.partial(layer_kernel, shards, requests, drafts),
        out_shape=jax.ShapeDtypeStruct((out_rows, depth), bf16),
        in_specs=[vmem] * 3 + [hbm] * 4,
        out_specs=vmem,
        scratch_shapes=[
            pltpu.VMEM(out_proj.shape, bf16),
            pltpu.VMEM(gate_w.shape, bf16),
            pltpu.VMEM(up_w.shape, bf16),
            pltpu.VMEM((2, units, piece), bf16),
            pltpu.VMEM((shards,) + attn.shape, bf16),
            pltpu.VMEM((shards, 1, width), f32),
            pltpu.VMEM((shards, rows, width), bf16),
            pltpu.VMEM((rows, depth), bf16),
            pltpu.VMEM((rows, depth), f32),
            pltpu.VMEM((CORES * out_rows, depth), f32),
            pltpu.VMEM((1, depth), f32),
            pltpu.VMEM((rows, units), bf16),
            pltpu.VMEM((16, piece), f32),
            pltpu.VMEM((16, piece), f32),
            pltpu.VMEM(slots, bf16),
            pltpu.VMEM(slots, bf16),
            pltpu.VMEM(slots, bf16),
            pltpu.VMEM(slots, bf16),
            dma((3 + depth // piece,)),
            dma((4, chips)),
            dma((4, chips)),
            dma((4, chips)),
            dma((2,)),
            dma((2, chips)),
        ],
        compiler_params=pltpu.CompilerParams(
            collective_id=0, has_side_effects=True, vmem_limit_bytes=60 * 1024 * 1024
        ),
        cost_estimate=pl.CostEstimate(
            flops=2 * rows * (depth * width + 3 * depth * units),
            bytes_accessed=2 * (depth * width + 3 * depth * units),
            transcendentals=rows * units,
        ),
    )(attn, residual_in, norm_gain.astype(f32).reshape(1, width), *weights)

def on_device(
    shards,
    residual_in,
    queries,
    key_cache,
    value_cache,
    new_keys,
    new_values,
    cache_len,
    tree_mask,
    out_proj,
    norm_gain,
    gate_w,
    up_w,
    down_w,
):
    blocks = queries.shape[0]
    drafts = queries.shape[1]
    requests = cache_len.shape[0]
    first_pair = lax.axis_index("shard") * blocks
    pair_index = first_pair + jnp.arange(blocks, dtype=jnp.int32)
    req_index = pair_index % requests
    req_pick = (req_index[:, None] == jnp.arange(requests, dtype=jnp.int32)[None, :]).astype(
        jnp.int32
    )
    lengths = jnp.sum(req_pick * cache_len[None, :], axis=1)
    tree_rows = jnp.einsum("br,rij->bij", req_pick, tree_mask)
    head_rows = queries.reshape(blocks, drafts, G, HD)
    score_scale = 1.0 / math.sqrt(HD)
    cache_scores = (
        jnp.einsum("bdgk,blk->bdgl", head_rows, key_cache, preferred_element_type=jnp.float32)
        * score_scale
    )
    draft_scores = (
        jnp.einsum("bdgk,bek->bdge", head_rows, new_keys, preferred_element_type=jnp.float32)
        * score_scale
    )
    valid_keys = jnp.arange(key_cache.shape[1], dtype=jnp.int32)[None, :] < lengths[:, None]
    cache_scores = jnp.where(valid_keys[:, None, None, :], cache_scores, -1e30)
    draft_scores = jnp.where(tree_rows[:, :, None, :] > 0, draft_scores, -1e30)
    peak_score = jnp.maximum(jnp.max(cache_scores, axis=-1), jnp.max(draft_scores, axis=-1))
    cache_weights = jnp.where(
        valid_keys[:, None, None, :], jnp.exp(cache_scores - peak_score[..., None]), 0.0
    )
    draft_weights = jnp.where(
        tree_rows[:, :, None, :] > 0, jnp.exp(draft_scores - peak_score[..., None]), 0.0
    )
    denom = jnp.sum(cache_weights, axis=-1) + jnp.sum(draft_weights, axis=-1)
    weighted = jnp.einsum(
        "bdgl,blk->bdgk",
        cache_weights.astype(jnp.bfloat16),
        value_cache,
        preferred_element_type=jnp.float32,
    )
    weighted = weighted + jnp.einsum(
        "bdge,bek->bdgk",
        draft_weights.astype(jnp.bfloat16),
        new_values,
        preferred_element_type=jnp.float32,
    )
    attn = (weighted / denom[..., None]).astype(jnp.bfloat16).reshape(blocks, drafts, G * HD)
    return rest_of_layer(
        shards,
        requests,
        drafts,
        attn.reshape(blocks * drafts, G * HD),
        residual_in,
        norm_gain,
        out_proj,
        gate_w,
        up_w,
        down_w,
    )


def solution(mesh):
    placed = (
        P("groups", "shard"),
        P(("groups", "shard"), None, None),
        P(("groups", "shard"), None, None),
        P(("groups", "shard"), None, None),
        P(("groups", "shard"), None, None),
        P(("groups", "shard"), None, None),
        P("groups"),
        P("groups", None, None),
        P(None, "shard"),
        P("shard"),
        P(None, "shard"),
        P(None, "shard"),
        P("shard", None),
    )
    return jax.shard_map(
        functools.partial(on_device, mesh.shape["shard"]),
        mesh=mesh,
        in_specs=placed,
        out_specs=P(("groups", "shard"), None),
        check_vma=False,
    )
```

time: 218 us -> 114 us (0.52)
  blocking collectives: 85.2 us -> 0 us
  waiting for transfers between devices: 62.6 us -> 0 us
  Pallas kernels: 0 us -> 50.6 us
  local copies, waits for them, and re-layouts: 6.35 us -> 55.1 us
  matrix products: 48.3 us -> 4.71 us
  between operations: 13.6 us -> 0.09 us
    unnamed x2 -> x0, waiting for transfers between devices: 62.6 us -> none
    pallas_call x0 -> x1, Pallas kernels: none -> 50.6 us  [rest_of_layer(): pl.pallas_call(functools.partial(layer_kernel, shards, requests, drafts),...]
    unnamed x22 -> x13, local copies, waits for them, and re-layouts: 5.01 us -> 53.8 us
    all_gather x2 -> x0, blocking collectives: 45.1 us -> none  [the longest x1 25.2 us: on_device(): share_slice = lax.all_gather(attn, 'shard', axis=0, tiled=True)]
    dot_general x5 -> x0, matrix products: 44.6 us -> none  [the longest x1 16 us: on_device(): lax.dot_general(down_w, hidden, (((0,), (1,)), ((), ())), preferred_eleme...]
    psum x1 -> x0, blocking collectives: 29.8 us -> none  [on_device(): squares = lax.psum(jnp.sum(wide_local * wide_local, axis=1), 'shard')]
    all_to_all x1 -> x0, blocking collectives: 10.2 us -> none  [on_device(): lax.all_to_all(finished, 'shard', split_axis=0, concat_axis=1, tiled=True)]
  transfers between devices with their start and end apart: 1 -> 0, of which waited for: 1 -> 0; matrix products, arithmetic and copies ran while one was open for 0% -> 0% of each run, Pallas kernels for 0% -> 0%
where the time goes in v1:
time: 114 us; the launch traced here: 112 us
  local copies, waits for them, and re-layouts  55.1 us (48%)
  Pallas kernels  50.6 us (44%)
  matrix products  4.71 us (4%)
  other arithmetic  1.77 us (2%)
    unnamed x13, local copies, waits for them, and re-layouts  53.8 us
    pallas_call x1, Pallas kernels, rest_of_layer(): pl.pallas_call(functools.partial(layer_kernel, shards, requests, drafts),...  50.6 us

profile of v1, /device:TPU:0, one launch (start us, length us, event | category | flops | bytes accessed | tf_op | source)
XLA Modules:
  0.0 112.3 jit_solution(14473157603133127447)
XLA Ops:
  0.0 0.0 copy-start
  0.0 1.0 select_reduce_fusion
  1.0 1.2 %reshape.57.gain_ref = f32[1,320]{1,0:T(1,128)} reshape(bf16[320]{0:T(512)(128)(2,1)} %param.22) | data formatting | bytes 1920 | tf_op jit(solution)/shard_map/reshape | solution.py:329
  2.2 1.0 convolution_compare_fusion
  3.2 0.1 copy.25
  3.3 0.1 iota_compare_fusion
  3.4 1.0 fusion.32
  4.4 0.0 copy-done
  4.4 0.0 copy-start.2
  4.4 1.9 %fusion.31 = (f32[2,16,5]{1,2,0:T(8,128)S(1)}, f32[2,16,5,4096]{3,1,2,0:T(8,128)S(1)}) fusion(bf16[2,4096,128]{2,1,0:T(8,128)(2,1)S(1)} %copy-done, pred[2,4096]{1,0:T(4,128)(4,1)S(1)} %iota_compare_fusion, bf16[2,16,640]{2,1,0:T(8,128)(2,1)} %param.14), kind=kOutput, calls=%fused_computation.42 | convolution fusion | flops 169738080 | bytes 4768384 | tf_op jit(solution)/shard_map/bdgk,blk->bdgl/dot_general | solution.py:361
  6.3 0.6 fusion.1
  6.9 0.0 copy-done.2
  7.0 0.0 copy-start.3
  7.0 0.7 fusion.3
  7.6 0.0 copy-done.3
  7.7 0.2 fusion.12
  7.9 0.6 copy.54
  8.5 5.8 %copy.29.wo_hbm = bf16[5120,320]{1,0:T(8,128)(2,1)} copy(bf16[5120,320]{0,1:T(8,128)(2,1)} %param.21) | data formatting | bytes 6553600 | tf_op args[8]
  14.4 22.9 %copy.30.gate_hbm = bf16[5120,1728]{1,0:T(8,128)(2,1)} copy(bf16[5120,1728]{0,1:T(8,128)(2,1)} %param.23) | data formatting | bytes 35389440 | tf_op args[10]
  37.3 23.0 %copy.31.up_hbm = bf16[5120,1728]{1,0:T(8,128)(2,1)} copy(bf16[5120,1728]{0,1:T(8,128)(2,1)} %param.24) | data formatting | bytes 35389440 | tf_op args[11]
  60.3 0.0 copy-start.1
  60.3 50.6 %shard_map.127 = bf16[4,5120]{1,0:T(4,128)(2,1)} custom-call(bf16[32,640]{1,0:T(8,128)(2,1)} %bitcast.49, bf16[64,320]{1,0:T(8,128)(2,1)} %resid_ref.1, f32[1,320]{1,0:T(1,128)} %reshape.57.gain_ref, bf16[5120,320]{1,0:T(8,128)(2,1)} %copy.29.wo_hbm, bf16[5120,1728]{1,0:T(8,128)(2,1)} %copy.30.gate_hbm, bf16[5120,1728]{1,0:T(8,128)(2,1)} %copy.31.up_hbm, ...), custom_call_target="tpu_custom_call" | custom-call | flops 3607101440 | bytes 56360960 | tf_op jit(solution)/shard_map/pallas_call | solution.py:290
  110.8 1.4 %copy.56 = bf16[4,5120]{1,0:T(4,128)(2,1)} copy(bf16[4,5120]{1,0:T(4,128)(2,1)} %shard_map.127) | data formatting | bytes 81920
  112.2 0.0 copy-done.1
  (5 shorter events, 0.1 us)
Async XLA Ops:
  0.0 4.4 %copy-start = (bf16[2,4096,128]{2,1,0:T(8,128)(2,1)S(1)}, bf16[2,4096,128]{2,1,0:T(8,128)(2,1)}, u32[]{:S(2)}) copy-start(bf16[2,4096,128]{2,1,0:T(8,128)(2,1)} %param.15) | copy-start | bytes 6291460
  4.4 2.6 %copy-start.2 = (bf16[2,4096,128]{2,1,0:T(8,128)(2,1)S(1)}, bf16[2,4096,128]{2,1,0:T(8,128)(2,1)}, u32[]{:S(2)}) copy-start(bf16[2,4096,128]{2,1,0:T(8,128)(2,1)} %param.16) | copy-start | bytes 6291460
  7.0 0.7 copy-start.3
  60.3 52.0 %copy-start.1 = (bf16[2,4096,128]{2,1,0:T(8,128)(2,1)S(1)}, bf16[2,4096,128]{2,1,0:T(8,128)(2,1)}, u32[]{:S(2)}) copy-start(bf16[2,4096,128]{2,1,0:T(8,128)(2,1)} %param.15) | copy-start | bytes 6291460

commit v2 on v1

--- a/solution.py
+++ b/solution.py
@@ -25,6 +25,10 @@
         device_id={"shard": target},
         device_id_type=pl.DeviceIdType.MESH,
     )
+
+
+def dot_transposed(a, b):
+    return lax.dot_general(a, b, (((1,), (1,)), ((), ())), preferred_element_type=jnp.float32)
 
 
 def layer_kernel(
@@ -167,7 +171,7 @@
             request * drafts : (request + 1) * drafts, head * head_width : (head + 1) * head_width
         ] = attn_slots[p // blocks, (p % blocks) * drafts : (p % blocks + 1) * drafts, :]
     wo_copy.wait()
-    mixed = jnp.dot(low_rows[...], wo[...], preferred_element_type=jnp.float32)
+    mixed = dot_transposed(low_rows[...], wo[...])
     stream_slots[me] = (resid_ref[...].astype(jnp.float32) + mixed).astype(jnp.bfloat16)
     gather_start(stream_slots, stream_sems)
     gather_finish(gain_slots, gain_sems)
@@ -189,13 +193,11 @@
 
     gate_copy.wait()
     up_copy.wait()
-    units = gate.shape[1]
+    units = gate.shape[0]
     for first in range(0, units, 512):
         last = min(first + 512, units)
-        gate_acts = jnp.dot(
-            low_rows[...], gate[:, first:last], preferred_element_type=jnp.float32
-        )
-        up_acts = jnp.dot(low_rows[...], up[:, first:last], preferred_element_type=jnp.float32)
+        gate_acts = dot_transposed(low_rows[...], gate[first:last, :])
+        up_acts = dot_transposed(low_rows[...], up[first:last, :])
         hidden[:, first:last] = (jax.nn.silu(gate_acts) * up_acts).astype(jnp.bfloat16)
 
     for q in range(total_pieces):
@@ -278,8 +280,8 @@
 def rest_of_layer(shards, requests, drafts, attn, residual_in, norm_gain, *weights):
     rows, width = residual_in.shape
     out_proj, gate_w, up_w, down_w = weights
-    depth = out_proj.shape[0]
-    units = gate_w.shape[1]
+    depth = out_proj.shape[1]
+    units = gate_w.shape[0]
     chips = shards // CORES
     out_rows = rows // shards
     piece = depth * out_rows // 16
@@ -396,9 +398,9 @@
         attn.reshape(blocks * drafts, G * HD),
         residual_in,
         norm_gain,
-        out_proj,
-        gate_w,
-        up_w,
+        out_proj.T,
+        gate_w.T,
+        up_w.T,
         down_w,
     )
 

time: 114 us -> 69.4 us (0.61); the launches traced: 112 us -> 69 us
  local copies, waits for them, and re-layouts: 55.1 us -> 3.28 us
  Pallas kernels: 50.6 us -> 55.9 us
  other arithmetic: 1.77 us -> 3.64 us
  matrix products: 4.71 us -> 6.06 us
    unnamed x13 -> x16, local copies, waits for them, and re-layouts: 53.8 us -> 2.59 us
    pallas_call x1, Pallas kernels: 50.6 us -> 55.9 us  [rest_of_layer(): pl.pallas_call(functools.partial(layer_kernel, shards, requests, drafts),...]
    reduce_sum x2, other arithmetic: 0.67 us -> 2.54 us  [on_device(): denom = jnp.sum(cache_weights, axis=-1) + jnp.sum(draft_weights, axis=-1)]
    dot_general x1, matrix products: 0.67 us -> 2.28 us  [on_device(): jnp.einsum('bdgl,blk->bdgk', cache_weights.astype(jnp.bfloat16), value_ca...]
    dot_general x1, matrix products: 1.85 us -> 3.13 us  [on_device(): jnp.einsum('bdgk,blk->bdgl', head_rows, key_cache, preferred_element_type...]
where the time goes in v2:
time: 69.4 us; the launch traced here: 69 us
  Pallas kernels  55.9 us (81%)
  matrix products  6.06 us (9%)
  other arithmetic  3.64 us (5%)
  local copies, waits for them, and re-layouts  3.28 us (5%)
    pallas_call x1, Pallas kernels, rest_of_layer(): pl.pallas_call(functools.partial(layer_kernel, shards, requests, drafts),...  55.9 us
    dot_general x1, matrix products, on_device(): jnp.einsum('bdgk,blk->bdgl', head_rows, key_cache, preferred_element_type...  3.13 us
    unnamed x16, local copies, waits for them, and re-layouts  2.59 us
    reduce_sum x2, other arithmetic, on_device(): denom = jnp.sum(cache_weights, axis=-1) + jnp.sum(draft_weights, axis=-1)  2.54 us
    dot_general x1, matrix products, on_device(): jnp.einsum('bdgl,blk->bdgk', cache_weights.astype(jnp.bfloat16), value_ca...  2.28 us

profile of v2, /device:TPU:0, one launch (start us, length us, event | category | flops | bytes accessed | tf_op | source)
XLA Modules:
  0.0 69.0 jit_solution(15834573816696530914)
XLA Ops:
  0.0 0.0 copy-start
  0.0 0.0 copy-start.2
  0.0 0.0 copy-start.5
  0.0 0.0 copy-start.3
  0.0 1.0 %select_reduce_fusion = s32[2]{0:T(128)S(1)} fusion(s32[4]{0:T(128)} %param.19, s32[2]{0:T(128)S(1)} %and_select_fusion), kind=kLoop, calls=%fused_computation.36 | loop fusion | flops 22 | bytes 32 | tf_op jit(solution)/shard_map/reduce_sum | solution.py:358
  1.0 0.1 iota_compare_fusion
  1.1 0.5 copy-done
  1.6 3.1 %fusion.31 = (f32[2,16,5]{1,2,0:T(8,128)S(1)}, f32[2,16,5,4096]{3,1,2,0:T(8,128)}) fusion(bf16[2,4096,128]{2,1,0:T(8,128)(2,1)S(1)} %copy-done, pred[2,4096]{1,0:T(4,128)(4,1)S(1)} %iota_compare_fusion, bf16[2,16,640]{2,1,0:T(8,128)(2,1)} %param.14), kind=kOutput, calls=%fused_computation.42 | convolution fusion | flops 169738080 | bytes 4768384 | tf_op jit(solution)/shard_map/bdgk,blk->bdgl/dot_general | solution.py:363
  4.8 0.0 copy-done.5
  4.8 0.2 convolution_compare_fusion
  5.0 0.1 copy.22
  5.1 0.0 copy-done.2
  5.1 0.0 copy-done.3
  5.1 0.0 copy-start.1
  5.1 0.2 fusion.32
  5.4 2.5 %fusion.1 = f32[2,16,5]{1,2,0:T(8,128)S(1)} fusion(f32[2,16,5,4096]{3,1,2,0:T(8,128)} %get-tuple-element.6, f32[2,16,5]{1,2,0:T(8,128)S(1)} %max.7, pred[2,4096]{1,0:T(4,128)(4,1)S(1)} %iota_compare_fusion), kind=kLoop, calls=%fused_computation.3 | loop fusion | flops 1965920 | bytes 2630912 | tf_op jit(solution)/shard_map/reduce_sum | solution.py:380
  7.9 0.0 copy-start.6
  7.9 0.0 copy-done.1
  7.9 0.0 copy-start.4
  7.9 2.3 %fusion.3 = f32[2,16,5,128]{3,1,2,0:T(8,128)S(1)} fusion(bf16[2,4096,128]{2,1,0:T(8,128)(2,1)} %param.16, f32[2,16,5,4096]{3,1,2,0:T(8,128)S(1)} %copy-done.1, f32[2,16,5]{1,2,0:T(8,128)S(1)} %max.7, pred[2,4096]{1,0:T(4,128)(4,1)S(1)} %iota_compare_fusion), kind=kOutput, calls=%fused_computation.5 | convolution fusion | flops 169738240 | bytes 4809344 | tf_op jit(solution)/shard_map/bdgl,blk->bdgk/dot_general | solution.py:381
  10.2 0.0 copy-done.6
  10.2 0.2 fusion.12
  10.5 0.6 copy.48
  11.1 0.0 copy-done.4
  11.1 0.6 reshape.57.gain_ref
  11.7 55.9 %shard_map.127 = bf16[4,5120]{1,0:T(4,128)(2,1)} custom-call(bf16[32,640]{1,0:T(8,128)(2,1)} %bitcast.55, bf16[64,320]{1,0:T(8,128)(2,1)} %resid_ref.1, f32[1,320]{1,0:T(1,128)} %reshape.57.gain_ref, bf16[320,5120]{1,0:T(8,128)(2,1)} %bitcast.53, bf16[1728,5120]{1,0:T(8,128)(2,1)} %bitcast.51, bf16[1728,5120]{1,0:T(8,128)(2,1)} %bitcast.52, ...), custom_call_target="tpu_custom_call" | custom-call | flops 3607101440 | bytes 56360960 | tf_op jit(solution)/shard_map/pallas_call | solution.py:292
  67.6 1.4 %copy.50 = bf16[4,5120]{1,0:T(4,128)(2,1)} copy(bf16[4,5120]{1,0:T(4,128)(2,1)} %shard_map.127) | data formatting | bytes 81920
  (5 shorter events, 0.1 us)
Async XLA Ops:
  0.0 1.6 %copy-start = (bf16[2,4096,128]{2,1,0:T(8,128)(2,1)S(1)}, bf16[2,4096,128]{2,1,0:T(8,128)(2,1)}, u32[]{:S(2)}) copy-start(bf16[2,4096,128]{2,1,0:T(8,128)(2,1)} %param.15) | copy-start | bytes 6291460
  0.0 5.1 %copy-start.2 = (bf16[2,16,640]{2,1,0:T(8,128)(2,1)S(1)}, bf16[2,16,640]{2,1,0:T(8,128)(2,1)}, u32[]{:S(2)}) copy-start(bf16[2,16,640]{2,1,0:T(8,128)(2,1)} %param.14) | copy-start | bytes 122884
  0.0 4.7 %copy-start.5 = (s32[4,16,16]{2,1,0:T(8,128)S(1)}, s32[4,16,16]{2,1,0:T(8,128)}, u32[]{:S(2)}) copy-start(s32[4,16,16]{2,1,0:T(8,128)} %param.20) | copy-start | bytes 12292
  0.0 5.1 %copy-start.3 = (bf16[2,16,128]{2,1,0:T(8,128)(2,1)S(1)}, bf16[2,16,128]{2,1,0:T(8,128)(2,1)}, u32[]{:S(2)}) copy-start(bf16[2,16,128]{2,1,0:T(8,128)(2,1)} %param.17) | copy-start | bytes 24580
  5.1 2.8 %copy-start.1 = (f32[2,16,5,4096]{3,1,2,0:T(8,128)S(1)}, f32[2,16,5,4096]{3,1,2,0:T(8,128)}, u32[]{:S(2)}) copy-start(f32[2,16,5,4096]{3,1,2,0:T(8,128)} %get-tuple-element.6) | copy-start | bytes 7864324
  7.9 2.3 %copy-start.6 = (bf16[2,16,128]{2,1,0:T(8,128)(2,1)S(1)}, bf16[2,16,128]{2,1,0:T(8,128)(2,1)}, u32[]{:S(2)}) copy-start(bf16[2,16,128]{2,1,0:T(8,128)(2,1)} %param.18) | copy-start | bytes 24580
  7.9 3.2 %copy-start.4 = (bf16[320]{0:T(512)(128)(2,1)S(1)}, bf16[320]{0:T(512)(128)(2,1)}, u32[]{:S(2)}) copy-start(bf16[320]{0:T(512)(128)(2,1)} %param.22) | copy-start | bytes 1924

commit v3 on v2

--- a/solution.py
+++ b/solution.py
@@ -219,14 +219,16 @@
             )
         return block[...]
 
-    def give(c, carry):
+    def exchange(c):
+        return remote(pair_out.at[c], pair_in.at[c], pair_sems.at[0, c], pair_sems.at[1, c], pair)
+
+    def give(j, carry):
+        c = (chip + j) % chips
         pair_out[c] = take(c, other_block, 1 - core).astype(jnp.bfloat16)
+        exchange(c).start()
         return carry
 
-    lax.fori_loop(0, chips, give, 0)
-    pair_copy = remote(pair_out, pair_in, pair_sems.at[0], pair_sems.at[1], pair)
-    pair_copy.start()
-    pair_copy.wait()
+    lax.fori_loop(1, chips + 1, give, 0)
 
     def scatter(j):
         target = (chip + j) % chips
@@ -240,12 +242,14 @@
 
     def combine(j, carry):
         target = (chip + j) % chips
+        exchange(target).wait_recv()
         summed = take(target, mine_block, core) + pair_in[target].astype(jnp.float32)
         send_blocks[target] = summed.astype(jnp.bfloat16)
         scatter(j).start()
         return carry
 
     lax.fori_loop(1, chips, combine, 0)
+    exchange(chip).wait_recv()
     total = take(chip, mine_block, core) + pair_in[chip].astype(jnp.float32)
 
     def add(j, total):
@@ -269,9 +273,11 @@
 
     def drain(j, carry):
         scatter(j).wait_send()
+        exchange((chip + j) % chips).wait_send()
         return carry
 
     lax.fori_loop(1, chips, drain, 0)
+    exchange(chip).wait_send()
     gather_drain(attn_slots, attn_sems)
     gather_drain(gain_slots, gain_sems)
     gather_drain(stream_slots, stream_sems)
@@ -317,7 +323,7 @@
             dma((4, chips)),
             dma((4, chips)),
             dma((4, chips)),
-            dma((2,)),
+            dma((2, chips)),
             dma((2, chips)),
         ],
         compiler_params=pltpu.CompilerParams(

time: 69.4 us -> 68.9 us (level)
  no operation moved by 1% of the time
where the time goes in v3:
time: 68.9 us; the launch traced here: 68.6 us
  Pallas kernels  55.5 us (81%)
  matrix products  6.06 us (9%)
  other arithmetic  3.64 us (5%)
  local copies, waits for them, and re-layouts  3.28 us (5%)
    pallas_call x1, Pallas kernels, rest_of_layer(): pl.pallas_call(functools.partial(layer_kernel, shards, requests, drafts),...  55.5 us
    dot_general x1, matrix products, on_device(): jnp.einsum('bdgk,blk->bdgl', head_rows, key_cache, preferred_element_type...  3.13 us
    unnamed x16, local copies, waits for them, and re-layouts  2.59 us
    reduce_sum x2, other arithmetic, on_device(): denom = jnp.sum(cache_weights, axis=-1) + jnp.sum(draft_weights, axis=-1)  2.54 us
    dot_general x1, matrix products, on_device(): jnp.einsum('bdgl,blk->bdgk', cache_weights.astype(jnp.bfloat16), value_ca...  2.28 us

profile of v3, /device:TPU:0, one launch (start us, length us, event | category | flops | bytes accessed | tf_op | source)
XLA Modules:
  0.0 68.6 jit_solution(3527953883802289201)
XLA Ops:
  0.0 0.0 copy-start
  0.0 0.0 copy-start.2
  0.0 0.0 copy-start.5
  0.0 0.0 copy-start.3
  0.0 1.0 %select_reduce_fusion = s32[2]{0:T(128)S(1)} fusion(s32[4]{0:T(128)} %param.19, s32[2]{0:T(128)S(1)} %and_select_fusion), kind=kLoop, calls=%fused_computation.36 | loop fusion | flops 22 | bytes 32 | tf_op jit(solution)/shard_map/reduce_sum | solution.py:364
  1.0 0.1 iota_compare_fusion
  1.1 0.5 copy-done
  1.6 3.1 %fusion.31 = (f32[2,16,5]{1,2,0:T(8,128)S(1)}, f32[2,16,5,4096]{3,1,2,0:T(8,128)}) fusion(bf16[2,4096,128]{2,1,0:T(8,128)(2,1)S(1)} %copy-done, pred[2,4096]{1,0:T(4,128)(4,1)S(1)} %iota_compare_fusion, bf16[2,16,640]{2,1,0:T(8,128)(2,1)} %param.14), kind=kOutput, calls=%fused_computation.42 | convolution fusion | flops 169738080 | bytes 4768384 | tf_op jit(solution)/shard_map/bdgk,blk->bdgl/dot_general | solution.py:369
  4.8 0.0 copy-done.5
  4.8 0.2 convolution_compare_fusion
  5.0 0.1 copy.22
  5.1 0.0 copy-done.2
  5.1 0.0 copy-done.3
  5.1 0.0 copy-start.1
  5.1 0.2 fusion.32
  5.4 2.5 %fusion.1 = f32[2,16,5]{1,2,0:T(8,128)S(1)} fusion(f32[2,16,5,4096]{3,1,2,0:T(8,128)} %get-tuple-element.6, f32[2,16,5]{1,2,0:T(8,128)S(1)} %max.7, pred[2,4096]{1,0:T(4,128)(4,1)S(1)} %iota_compare_fusion), kind=kLoop, calls=%fused_computation.3 | loop fusion | flops 1965920 | bytes 2630912 | tf_op jit(solution)/shard_map/reduce_sum | solution.py:386
  7.9 0.0 copy-start.6
  7.9 0.0 copy-done.1
  7.9 0.0 copy-start.4
  7.9 2.3 %fusion.3 = f32[2,16,5,128]{3,1,2,0:T(8,128)S(1)} fusion(bf16[2,4096,128]{2,1,0:T(8,128)(2,1)} %param.16, f32[2,16,5,4096]{3,1,2,0:T(8,128)S(1)} %copy-done.1, f32[2,16,5]{1,2,0:T(8,128)S(1)} %max.7, pred[2,4096]{1,0:T(4,128)(4,1)S(1)} %iota_compare_fusion), kind=kOutput, calls=%fused_computation.5 | convolution fusion | flops 169738240 | bytes 4809344 | tf_op jit(solution)/shard_map/bdgl,blk->bdgk/dot_general | solution.py:387
  10.2 0.0 copy-done.6
  10.2 0.2 fusion.12
  10.5 0.6 copy.48
  11.1 0.0 copy-done.4
  11.1 0.6 reshape.57.gain_ref
  11.7 55.5 %shard_map.127 = bf16[4,5120]{1,0:T(4,128)(2,1)} custom-call(bf16[32,640]{1,0:T(8,128)(2,1)} %bitcast.55, bf16[64,320]{1,0:T(8,128)(2,1)} %resid_ref.1, f32[1,320]{1,0:T(1,128)} %reshape.57.gain_ref, bf16[320,5120]{1,0:T(8,128)(2,1)} %bitcast.53, bf16[1728,5120]{1,0:T(8,128)(2,1)} %bitcast.51, bf16[1728,5120]{1,0:T(8,128)(2,1)} %bitcast.52, ...), custom_call_target="tpu_custom_call" | custom-call | flops 3607101440 | bytes 56360960 | tf_op jit(solution)/shard_map/pallas_call | solution.py:298
  67.2 1.4 %copy.50 = bf16[4,5120]{1,0:T(4,128)(2,1)} copy(bf16[4,5120]{1,0:T(4,128)(2,1)} %shard_map.127) | data formatting | bytes 81920
  (5 shorter events, 0.1 us)
Async XLA Ops:
  0.0 1.6 %copy-start = (bf16[2,4096,128]{2,1,0:T(8,128)(2,1)S(1)}, bf16[2,4096,128]{2,1,0:T(8,128)(2,1)}, u32[]{:S(2)}) copy-start(bf16[2,4096,128]{2,1,0:T(8,128)(2,1)} %param.15) | copy-start | bytes 6291460
  0.0 5.1 %copy-start.2 = (bf16[2,16,640]{2,1,0:T(8,128)(2,1)S(1)}, bf16[2,16,640]{2,1,0:T(8,128)(2,1)}, u32[]{:S(2)}) copy-start(bf16[2,16,640]{2,1,0:T(8,128)(2,1)} %param.14) | copy-start | bytes 122884
  0.0 4.7 %copy-start.5 = (s32[4,16,16]{2,1,0:T(8,128)S(1)}, s32[4,16,16]{2,1,0:T(8,128)}, u32[]{:S(2)}) copy-start(s32[4,16,16]{2,1,0:T(8,128)} %param.20) | copy-start | bytes 12292
  0.0 5.1 %copy-start.3 = (bf16[2,16,128]{2,1,0:T(8,128)(2,1)S(1)}, bf16[2,16,128]{2,1,0:T(8,128)(2,1)}, u32[]{:S(2)}) copy-start(bf16[2,16,128]{2,1,0:T(8,128)(2,1)} %param.17) | copy-start | bytes 24580
  5.1 2.8 %copy-start.1 = (f32[2,16,5,4096]{3,1,2,0:T(8,128)S(1)}, f32[2,16,5,4096]{3,1,2,0:T(8,128)}, u32[]{:S(2)}) copy-start(f32[2,16,5,4096]{3,1,2,0:T(8,128)} %get-tuple-element.6) | copy-start | bytes 7864324
  7.9 2.3 %copy-start.6 = (bf16[2,16,128]{2,1,0:T(8,128)(2,1)S(1)}, bf16[2,16,128]{2,1,0:T(8,128)(2,1)}, u32[]{:S(2)}) copy-start(bf16[2,16,128]{2,1,0:T(8,128)(2,1)} %param.18) | copy-start | bytes 24580
  7.9 3.2 %copy-start.4 = (bf16[320]{0:T(512)(128)(2,1)S(1)}, bf16[320]{0:T(512)(128)(2,1)}, u32[]{:S(2)}) copy-start(bf16[320]{0:T(512)(128)(2,1)} %param.22) | copy-start | bytes 1924
